TPU v7x, 256 devices: a whole 4x4x8 slice. The times are simulated.
256 devices in a mesh: fsdp: 16 (over z_lo, y), tp: 16 (over z_hi, x, core).
Axes of the slice: x: 4, y: 4, z: 8 (z_hi: 2, z_lo: 4; z = z_hi * 4 + z_lo), core: 2. Of those that a mesh axis runs over, the one named last changes fastest.
Arguments:
- output_gradient: bfloat16 [8192, 8192], P('fsdp'), may hold values from -6 to 6
- gate_pre: bfloat16 [8192, 14336], P('fsdp', 'tp'), may hold values from -6 to 6
- up_pre: bfloat16 [8192, 14336], P('fsdp', 'tp'), may hold values from -6 to 6
- down_weight: bfloat16 [14336, 8192], P('tp', 'fsdp'), may hold values from -0.046875 to 0.046875
- a_mean: float32 [8, 14336], P(None, 'tp'), may hold values from -0.75 to 0.75
- a_sigma: float32 [8, 14336], P(None, 'tp'), may hold values from 0.02 to 0.1
- a_noise: float32 [8, 14336], P(None, 'tp'), may hold values from -6 to 6
- second_factor: float32 [8, 8192], replicated, may hold values from -0.3125 to 0.3125
- in_signs: int32 [8192, 14336], P('fsdp', 'tp'), may hold values from -1 to 1, as said below
- out_signs: int32 [8192, 8], P('fsdp'), may hold values from -1 to 1, as said below
Outputs:
- d_gate: bfloat16 [8192, 14336], P('fsdp', 'tp')
- d_up: bfloat16 [8192, 14336], P('fsdp', 'tp')
- d_mean: float32 [8, 14336], P(None, 'tp')
- d_sigma: float32 [8, 14336], P(None, 'tp')
- second_factor_gradient: float32 [8, 8192], P(None, 'tp')
Inputs may be any that keep to these rules, and one draw needn't show every extreme that they name: `in_signs`: every entry is -1 or +1. `out_signs`: every entry is -1 or +1.
All inputs are finite; a program needn't handle non-finite values.
Results may differ from a plain program's by a relative error of at most 0.0031.
Values may be sent and summed in bfloat16 or wider, within the bound.
A program may use at most 128 MiB of HBM per device.

v0:
```python
import math

import jax
import jax.numpy as jnp
from jax import lax
from jax.sharding import PartitionSpec as P

adapter_scale = 2.0


def contract_last(left_rows, right_rows):
    return lax.dot_general(
        left_rows, right_rows, (((1,), (1,)), ((), ())), preferred_element_type=jnp.float32
    )


def local(
    output_gradient,
    gate_pre,
    up_pre,
    down_weight,
    a_mean,
    a_sigma,
    a_noise,
    second_factor,
    in_signs,
    out_signs,
):
    highest_precision = lax.Precision.HIGHEST
    gate_wide = gate_pre.astype(jnp.float32)
    up_wide = up_pre.astype(jnp.float32)
    sigmoid_gate = jax.nn.sigmoid(gate_wide)
    hidden = (gate_wide * sigmoid_gate * up_wide).astype(jnp.bfloat16)
    spread = a_sigma * a_noise
    sign_in = in_signs.astype(jnp.float32)
    sign_out = out_signs.astype(jnp.float32)
    flipped = hidden * sign_in
    rank_local = jnp.dot(
        hidden, a_mean.T, precision=highest_precision, preferred_element_type=jnp.float32
    ) + sign_out * jnp.dot(
        flipped, spread.T, precision=highest_precision, preferred_element_type=jnp.float32
    )
    rank_values = lax.psum(rank_local, "tp")
    rank_gradient = adapter_scale * jnp.dot(
        output_gradient,
        second_factor.T,
        precision=highest_precision,
        preferred_element_type=jnp.float32,
    )
    tok_count = output_gradient.shape[0]
    base_grad = contract_last(
        output_gradient, lax.all_gather(down_weight, "fsdp", axis=1, tiled=True)
    )
    signed_grad = rank_gradient * sign_out
    hidden_grad = (
        base_grad
        + jnp.dot(
            rank_gradient, a_mean, precision=highest_precision, preferred_element_type=jnp.float32
        )
        + sign_in
        * jnp.dot(
            signed_grad, spread, precision=highest_precision, preferred_element_type=jnp.float32
        )
    )
    d_gate = (
        hidden_grad * up_wide * sigmoid_gate * (1.0 + gate_wide * (1.0 - sigmoid_gate))
    ).astype(jnp.bfloat16)
    d_up = (hidden_grad * gate_wide * sigmoid_gate).astype(jnp.bfloat16)
    out_width = output_gradient.shape[1] // lax.axis_size("tp")
    out_cols = lax.dynamic_slice_in_dim(
        output_gradient, lax.axis_index("tp") * out_width, out_width, 1
    )
    mean_part = jnp.dot(
        rank_gradient.T, hidden, precision=highest_precision, preferred_element_type=jnp.float32
    )
    sigma_part = jnp.dot(
        signed_grad.T, flipped, precision=highest_precision, preferred_element_type=jnp.float32
    )
    factor_part = jnp.dot(
        rank_values.T, out_cols, precision=highest_precision, preferred_element_type=jnp.float32
    )
    mean_sum, sigma_sum, factor_total = lax.psum((mean_part, sigma_part, factor_part), "fsdp")
    normalizing_count = 1.0 / math.sqrt(tok_count * lax.axis_size("fsdp"))
    d_mean = normalizing_count * mean_sum
    d_sigma = normalizing_count * a_noise * sigma_sum
    second_factor_gradient = normalizing_count * adapter_scale * factor_total
    return (d_gate, d_up, d_mean, d_sigma, second_factor_gradient)


def solution(mesh):
    placed = (
        P("fsdp", None),
        P("fsdp", "tp"),
        P("fsdp", "tp"),
        P("tp", "fsdp"),
        P(None, "tp"),
        P(None, "tp"),
        P(None, "tp"),
        P(),
        P("fsdp", "tp"),
        P("fsdp", None),
    )
    return jax.shard_map(
        local,
        mesh=mesh,
        in_specs=placed,
        out_specs=(P("fsdp", "tp"), P("fsdp", "tp"), P(None, "tp"), P(None, "tp"), P(None, "tp")),
        check_vma=False,
    )
```

profile of v0, /device:TPU:64, one launch (start us, length us, event | category | flops | bytes accessed | tf_op | source)
XLA Modules:
  0.0 438.7 jit_solution(13460722747519460938)
XLA Ops:
  7.2 0.0 copy-start
  7.2 0.0 all-gather.2.cloned.1.call-start
  7.2 0.7 all-gather.2.cloned.1.call-update
  7.9 0.0 all-reduce.3.cloned.1.call-start
  8.0 0.2 copy-done
  8.1 0.0 copy-start.5
  8.1 0.0 copy-start.4
  8.1 8.9 %convolution_multiply_fusion = f32[512,8]{0,1:T(8,128)S(1)} fusion(bf16[512,8192]{1,0:T(8,128)(2,1)} %param.10, f32[8,8192]{1,0:T(8,128)S(1)} %copy-done), kind=kOutput, calls=%fused_computation.22 | convolution fusion | flops 402657280 | bytes 8667136 | tf_op jit(solution)/shard_map/dot_general | solution.py:44
  17.1 0.0 copy-done.5
  17.1 0.0 copy-start.2
  17.1 0.0 copy-start.3
  17.1 0.0 copy-start.1
  17.1 2.9 fusion.20
  20.0 0.0 copy-done.4
  20.0 0.0 copy-done.2
  20.0 0.0 copy-done.3
  20.0 2.9 fusion.17
  22.9 151.8 %all-gather.2.cloned.1.call-done = bf16[896,8192]{1,0:T(8,128)(2,1)} async-done(((bf16[896,512]{1,0:T(8,128)(2,1)}), bf16[896,8192]{1,0:T(8,128)(2,1)}) %all-gather.2.cloned.1.call-update) | async-done | bytes 14680080 | tf_op jit(solution)/shard_map/all_gather | solution.py:52
  174.7 0.0 copy-done.1
  174.7 18.6 %fusion.9 = (bf16[512,896]{1,0:T(8,128)(2,1)}, bf16[512,896]{1,0:T(8,128)(2,1)}, bf16[512,896]{1,0:T(8,128)(2,1)S(1)}) fusion(bf16[512,896]{1,0:T(8,128)(2,1)} %param.11, bf16[512,896]{1,0:T(8,128)(2,1)} %param.12, f32[512,896]{1,0:T(8,128)} %fusion.17, s32[512,896]{1,0:T(8,128)S(1)} %copy-done.1, f32[512,896]{1,0:T(8,128)} %fusion.20, ...), kind=kOutput, calls=%fused_computation.15 | convolution fusion | flops 7526285312 | bytes 33161216 | tf_op jit(solution)/shard_map/dot_general | solution.py:12
  193.3 0.8 fusion.22
  194.1 1.8 fusion.11
  195.9 1.1 fusion.21
  197.0 1.8 fusion.13
  198.8 90.5 %psum.30 = f32[512,8]{0,1:T(8,128)S(1)} all-reduce(f32[512,8]{0,1:T(8,128)S(1)} %fusion.13), channel_id=1, replica_groups=mesh['fsdp'=16,'tp'=16] {'tp'}, use_global_device_ids=true, to_apply=%region_2.0 | all-reduce | flops 4096 | bytes 32768 | tf_op jit(solution)/shard_map/psum | solution.py:43
  289.3 2.0 fusion.14
  291.2 0.0 all-reduce.3.cloned.1.call-update
  291.2 137.9 %all-reduce.3.cloned.1.call-done = (f32[8,896]{1,0:T(8,128)}, f32[8,896]{1,0:T(8,128)}, f32[8,512]{1,0:T(8,128)}) async-done(((f32[8,896]{1,0:T(8,128)}, f32[8,896]{1,0:T(8,128)}, f32[8,512]{1,0:T(8,128)}), (f32[8,896]{1,0:T(8,128)}, f32[8,896]{1,0:T(8,128)}, f32[8,512]{1,0:T(8,128)})) %all-reduce.3.cloned.1.call-update) | async-done | bytes 73744 | tf_op jit(solution)/shard_map/psum | solution.py:82
  429.1 1.3 broadcast_multiply_fusion.1
  430.5 1.4 multiply_multiply_fusion
Async XLA Ops:
  7.2 1.0 copy-start
  7.2 167.5 %all-gather.2.cloned.1.call-start = ((), (), s32[]{:S(2)}) async-start(), calls=%async_computation | async-start | bytes 15597568 | tf_op jit(solution)/shard_map/all_gather | solution.py:52
  7.9 421.2 %all-reduce.3.cloned.1.call-start = ((), (), s32[]{:S(2)}) async-start(), calls=%async_computation.1 | async-start | bytes 147456 | tf_op jit(solution)/shard_map/psum | solution.py:82
  8.1 8.9 %copy-start.5 = (f32[8,896]{1,0:T(8,128)S(1)}, f32[8,896]{1,0:T(8,128)}, u32[]{:S(2)}) copy-start(f32[8,896]{1,0:T(8,128)} %param.14) | copy-start | bytes 86020
  8.1 11.9 %copy-start.4 = (f32[8,896]{1,0:T(8,128)S(1)}, f32[8,896]{1,0:T(8,128)}, u32[]{:S(2)}) copy-start(f32[8,896]{1,0:T(8,128)} %param.15) | copy-start | bytes 86020
  17.1 2.9 copy-start.2
  17.1 2.9 copy-start.3
  17.1 157.6 %copy-start.1 = (s32[512,896]{1,0:T(8,128)S(1)}, s32[512,896]{1,0:T(8,128)}, u32[]{:S(2)}) copy-start(s32[512,896]{1,0:T(8,128)} %param.18) | copy-start | bytes 5505028
Sparse Core Ops, SparseCore 0:
  9.8 164.8 all-gather.1
  291.4 137.7 all-reduce.2
where the time goes:
time: 445 us; the launch traced here: 439 us
  waiting for transfers between devices  290 us (65%)
  blocking collectives  90.5 us (20%)
  matrix products  40.7 us (9%)
  between operations  14.1 us (3%)
    all_gather x1, waiting for transfers between devices, local(): lax.all_gather(down_weight, 'fsdp', axis=1, tiled=True)  152 us
    psum x1, waiting for transfers between devices, local(): lax.psum((mean_part, sigma_part, factor_part), 'fsdp')  138 us
    psum x1, blocking collectives, local(): rank_values = lax.psum(rank_local, 'tp')  90.5 us
    dot_general x1, matrix products, contract_last(): lax.dot_general(left_rows, right_rows, (((1,), (1,)), ((), ())), preferre...  18.6 us
    dot_general x1, matrix products, local(): jnp.dot(output_gradient, second_factor.T, precision=highest_precision, pr...  8.92 us
  transfers between devices with their start and end apart: 2, of which 2 were waited for; matrix products, arithmetic and copies ran while one was open for 3% of the time, Pallas kernels for 0%

commit v1 on v0

v1 whole, which is shorter than its diff:
```python
import math

import jax
import jax.numpy as jnp
from jax import lax
from jax.experimental import pallas as pl
from jax.experimental.pallas import tpu as pltpu
from jax.sharding import PartitionSpec as P

MESH = pl.DeviceIdType.MESH
F32 = jnp.float32
BF16 = jnp.bfloat16
adapter_scale = 2.0

TOK = 512
WID = 512
HID = 896
CH = 128
NCH = HID // CH
HALF = 2048
RED = 2 * HID + WID


def nt(left, right):
    return lax.dot_general(left, right, (((1,), (1,)), ((), ())), preferred_element_type=F32)


def nn(left, right):
    return lax.dot_general(left, right, (((1,), (0,)), ((), ())), preferred_element_type=F32)


def thirds(value):
    first = value.astype(BF16).astype(F32)
    rest = value - first
    second = rest.astype(BF16).astype(F32)
    third = (rest - second).astype(BF16).astype(F32)
    return first, second, third


def kernel(
    og,
    gate,
    up,
    dw,
    a_mean,
    a_sigma,
    a_noise,
    factor,
    in_signs,
    out_signs,
    d_gate,
    d_up,
    d_mean,
    d_sigma,
    d_factor,
    DW,
    OGO,
    OGX,
    OGP,
    OGC,
    G,
    U,
    IS,
    H,
    HS,
    CA,
    CB,
    OWN,
    PACC,
    RSS,
    RSR,
    SF,
    LT,
    R1,
    R2,
    SO,
    RVS,
    RVR,
    RY,
    RZ,
    local_sem,
    send_dw,
    send_og,
    send_rs,
    send_rv,
    send_ry,
    send_rz,
    rz,
    ra,
    rb,
    rc,
    rp,
    rr,
    rv,
    ry,
    rzz,
):
    fi = lax.axis_index("fsdp")
    tj = lax.axis_index("tp")
    y, z = lax.rem(fi, 4), lax.div(fi, 4)
    c, x, zh = lax.rem(tj, 2), lax.rem(lax.div(tj, 2), 4), lax.div(tj, 8)
    par, h0 = lax.rem(z, 2), lax.div(z, 2)
    h1 = 1 - h0

    def at(px=x, py=y, pz=z, pzh=zh, pc=c):
        return (pz * 4 + py, (pzh * 4 + px) * 2 + pc)

    def ring(value, step):
        return lax.rem(value + step, 4)

    right, left = at(py=ring(y, 1)), at(py=ring(y, 3))
    pair = at(pz=z + 1 - 2 * par)
    across = at(pz=ring(z, 2))
    sibling = at(pc=1 - c)
    other_hi = at(pzh=1 - zh)
    ys = [at(py=ring(y, d)) for d in (1, 2, 3)]
    zs = [at(pz=ring(z, d)) for d in (1, 2, 3)]
    xs = [at(px=ring(x, d)) for d in (1, 2, 3)]

    barrier = pltpu.get_barrier_semaphore()
    partners = ys + zs + xs + [sibling, other_hi]
    for partner in partners:
        pl.semaphore_signal(barrier, inc=1, device_id=partner, device_id_type=MESH)

    own = h0 * 4 + y
    mirror = h1 * 4 + y

    local = [
        pltpu.make_async_copy(dw, DW.at[own], local_sem.at[0]),
        pltpu.make_async_copy(gate, G, local_sem.at[1]),
        pltpu.make_async_copy(up, U, local_sem.at[2]),
        pltpu.make_async_copy(in_signs, IS, local_sem.at[3]),
    ]
    for h in range(2):
        mine = pl.ds(pl.multiple_of((2 * h + par) * HALF, HALF), HALF)
        rest = pl.ds(pl.multiple_of((2 * h + 1 - par) * HALF, HALF), HALF)
        local.append(pltpu.make_async_copy(og.at[:, mine], OGO.at[h], local_sem.at[4 + 2 * h]))
        local.append(pltpu.make_async_copy(og.at[:, rest], OGX.at[h], local_sem.at[5 + 2 * h]))
    out_cols = pl.ds(pl.multiple_of(tj * WID, WID), WID)
    local.append(pltpu.make_async_copy(og.at[:, out_cols], OGC, local_sem.at[8]))
    for copy in local:
        copy.start()

    pl.semaphore_wait(barrier, len(partners))

    def send(src, dst, send_sem, recv_sem, device):
        pltpu.make_async_remote_copy(
            src_ref=src,
            dst_ref=dst,
            send_sem=send_sem,
            recv_sem=recv_sem,
            device_id=device,
            device_id_type=MESH,
        ).start()

    def landed(ref, sem):
        pltpu.make_async_copy(ref, ref, sem).wait()

    def piece(q, h):
        return OGP.at[h, pl.ds(pl.multiple_of(q * 64, 64), 64)]

    q_own = x * 2 + c

    def step_p(h):
        rows = pl.ds(pl.multiple_of(q_own * 64, 64), 64)
        cols = pl.ds(pl.multiple_of((2 * h + 1 - par) * HALF, HALF), HALF)
        send(og.at[rows, cols], piece(q_own, h), send_og, rp.at[q_own, h], pair)

    def step_x(h):
        landed(piece(q_own, h), rp.at[q_own, h])
        for device in xs + [sibling]:
            send(piece(q_own, h), piece(q_own, h), send_og, rp.at[q_own, h], device)

    def step_y(h):
        for d in (1, 3, 2):
            q = ring(x, d) * 2 + c
            landed(piece(q, h), rp.at[q, h])
            send(piece(q, h), piece(q, h), send_og, rp.at[q, h], sibling)

    def step_w(h):
        for px in range(4):
            q = px * 2 + 1 - c
            landed(piece(q, h), rp.at[q, h])

    def rows_of(slot, k, part=None):
        if part is None:
            return DW.at[slot, pl.ds(k * CH, CH)]
        return DW.at[slot, pl.ds(k * CH + part * (CH // 2), CH // 2)]

    def step_z(k):
        send(rows_of(own, k), rows_of(own, k), send_dw, rz.at[k], across)

    def step_a(k):
        send(rows_of(own, k), rows_of(own, k), send_dw, ra.at[0, k], right)
        send(rows_of(own, k), rows_of(own, k), send_dw, ra.at[1, k], left)

    def step_b(k):
        landed(rows_of(mirror, k), rz.at[k])
        send(rows_of(mirror, k), rows_of(mirror, k), send_dw, rb.at[0, k], right)
        send(rows_of(mirror, k), rows_of(mirror, k), send_dw, rb.at[1, k], left)

    def relay(sems, h, group, k):
        slot = h * 4 + ring(y, 3)
        landed(rows_of(slot, k), sems.at[0, k])
        send(rows_of(slot, k, 0), rows_of(slot, k, 0), send_dw, rc.at[0, group, k], right)
        slot = h * 4 + ring(y, 1)
        landed(rows_of(slot, k), sems.at[1, k])
        send(rows_of(slot, k, 1), rows_of(slot, k, 1), send_dw, rc.at[1, group, k], left)

    def step_c(k):
        relay(ra, h0, 0, k)

    def step_d(k):
        relay(rb, h1, 1, k)

    def step_e(k):
        for group, h in ((0, h0), (1, h1)):
            for part in range(2):
                landed(rows_of(h * 4 + ring(y, 2), k, part), rc.at[part, group, k])

    def matmul(k, count):
        rows = pl.ds(k * CH, count * CH)
        cols = slice(k * CH, (k + count) * CH)
        wide = slice(0, count * CH)
        PACC[:, wide] = jnp.zeros((TOK, count * CH), F32)

        def part(src, acc, acc_cols):
            def body(s, carry):
                kcols = pl.ds(pl.multiple_of(lax.rem(s, 4) * WID, WID), WID)
                acc[:, acc_cols] += nt(src[lax.div(s, 4), :, kcols], DW[s, rows, :])
                return carry

            lax.fori_loop(0, 8, body, 0)

        part(OGP, PACC, wide)
        for n in range(count):
            RSS[k + n] = PACC[:, n * CH : (n + 1) * CH].astype(BF16)
            send(RSS.at[k + n], RSR.at[k + n], send_rs, rr.at[k + n], pair)
        part(OGO, OWN, cols)

    def finish(k):
        cols = slice(k * CH, (k + 1) * CH)
        landed(RSR.at[k], rr.at[k])
        hidden_grad = OWN[:, cols] + RSR[k].astype(F32)
        d_gate[:, cols] = (hidden_grad * CA[:, cols]).astype(BF16)
        d_up[:, cols] = (hidden_grad * CB[:, cols]).astype(BF16)

    step_p(0)
    step_p(1)
    local[0].wait()
    for k in range(NCH):
        step_z(k)
        if k < 3:
            step_a(k)

    for n in (1, 2, 3):
        local[n].wait()

    def pre(k, carry):
        cols = pl.ds(pl.multiple_of(k * CH, CH), CH)
        g = G[:, cols].astype(F32)
        u = U[:, cols].astype(F32)
        s = jax.nn.sigmoid(g)
        hidden = (g * s * u).astype(BF16)
        H[:, cols] = hidden
        HS[:, cols] = (hidden.astype(F32) * IS[:, cols].astype(F32)).astype(BF16)
        CA[:, cols] = u * s * (1.0 + g * (1.0 - s))
        CB[:, cols] = g * s
        return carry

    lax.fori_loop(0, NCH, pre, 0)

    spread = a_sigma[...] * a_noise[...]
    am = thirds(a_mean[...])
    sp = thirds(spread)
    gap = jnp.zeros((8, HID), F32)
    R1[...] = jnp.concatenate([am[0], am[1], am[2]] + [gap] * 13, axis=0).astype(BF16)
    R2[...] = jnp.concatenate([gap] * 4 + [sp[0], sp[1], sp[2]] + [gap] * 9, axis=0).astype(BF16)
    eye = (
        lax.broadcasted_iota(jnp.int32, (8, 8), 0) == lax.broadcasted_iota(jnp.int32, (8, 8), 1)
    ).astype(F32)
    SO[...] = nt(eye, out_signs[...].astype(F32))
    both = (nt(H[...], R1[...]) + nt(HS[...], R2[...])).T
    RVS[0] = (both[0:8] + both[8:16] + both[16:24]) + SO[...] * (
        both[32:40] + both[40:48] + both[48:56]
    )
    send(RVS.at[0], RVR.at[0], send_rv.at[0], rv.at[0], sibling)

    step_c(0)
    step_a(3)
    step_b(0)
    step_x(0)

    sf = thirds(factor[...])
    SF[...] = jnp.concatenate(
        [sf[0], sf[1], sf[2]] + [jnp.zeros((8, 4 * HALF), F32)] * 13, axis=0
    ).astype(BF16)
    LTF = None
    for n in range(4, 9):
        local[n].wait()
    for h in range(2):
        mine = pl.ds(pl.multiple_of((2 * h + par) * HALF, HALF), HALF)
        rest = pl.ds(pl.multiple_of((2 * h + 1 - par) * HALF, HALF), HALF)
        term = nt(OGO[h], SF[:, mine]) + nt(OGX[h], SF[:, rest])
        LTF = term if LTF is None else LTF + term
    turned = LTF.T
    rank_grad = adapter_scale * (turned[0:8] + turned[8:16] + turned[16:24])
    signed = rank_grad * SO[...]
    rg = thirds(rank_grad)
    sg = thirds(signed)

    step_c(1)
    step_a(4)
    step_b(1)
    step_d(0)
    step_x(1)

    landed(RVR.at[0], rv.at[0])
    RVS[1] = RVS[0] + RVR[0]
    for d in (1, 2, 3):
        send(RVS.at[1], RVR.at[d], send_rv.at[d], rv.at[d], xs[d - 1])

    blank = jnp.zeros((8, TOK), F32)
    LT[...] = (
        jnp.concatenate(
            [rg[0], rg[0], rg[1], rg[1], rg[0], rg[2], blank, blank]
            + [sg[0], sg[0], sg[1], sg[1], sg[0], sg[2], blank, blank],
            axis=0,
        )
        .T.astype(BF16)
    )
    mean3 = nn(jnp.concatenate(list(rg) + [blank], axis=0).astype(BF16), H[...])
    sigma3 = nn(jnp.concatenate(list(sg) + [blank], axis=0).astype(BF16), HS[...])
    RY[y, :, 0:HID] = mean3[0:8] + mean3[8:16] + mean3[16:24]
    RY[y, :, HID : 2 * HID] = sigma3[0:8] + sigma3[8:16] + sigma3[16:24]
    R1[...] = jnp.concatenate(
        [am[0], am[1], am[0], am[1], am[2], am[0]] + [gap] * 10, axis=0
    ).astype(BF16)
    R2[...] = jnp.concatenate(
        [gap] * 8 + [sp[0], sp[1], sp[0], sp[1], sp[2], sp[0]] + [gap] * 2, axis=0
    ).astype(BF16)

    def rank_terms(k, carry):
        cols = pl.ds(pl.multiple_of(k * CH, CH), CH)
        OWN[:, cols] = nn(LT[...], R1[:, cols]) + IS[:, cols].astype(F32) * nn(LT[...], R2[:, cols])
        return carry

    lax.fori_loop(0, NCH, rank_terms, 0)

    step_y(0)
    step_c(2)
    step_a(5)
    step_b(2)
    step_d(1)

    for d in (1, 2, 3):
        landed(RVR.at[d], rv.at[d])
    RVS[2] = RVS[1] + RVR[1] + RVR[2] + RVR[3]
    send(RVS.at[2], RVR.at[4], send_rv.at[4], rv.at[4], other_hi)

    step_y(1)
    step_w(0)
    step_c(3)
    step_a(6)
    step_b(3)
    step_d(2)
    step_w(1)

    landed(RVR.at[4], rv.at[4])
    ranks = thirds(RVS[2] + RVR[4])
    factor3 = nn(jnp.concatenate(list(ranks) + [blank], axis=0).astype(BF16), OGC[...])
    RY[y, :, 2 * HID :] = factor3[0:8] + factor3[8:16] + factor3[16:24]
    for d in (1, 2, 3):
        send(RY.at[y], RY.at[y], send_ry.at[d - 1], ry.at[d - 1], ys[d - 1])

    step_e(0)
    step_e(1)
    matmul(0, 2)

    step_c(4)
    step_b(4)
    step_d(3)

    for d in (1, 2, 3):
        landed(RY.at[ring(y, 4 - d)], ry.at[d - 1])
    RZ[z] = ((RY[0] + RY[1]) + RY[2]) + RY[3]
    for d in (1, 2, 3):
        send(RZ.at[z], RZ.at[z], send_rz.at[d - 1], rzz.at[d - 1], zs[d - 1])

    step_e(2)
    step_e(3)
    matmul(2, 2)
    step_c(5)
    step_b(5)
    step_d(4)
    finish(0)
    finish(1)

    for d in (1, 2, 3):
        landed(RZ.at[ring(z, 4 - d)], rzz.at[d - 1])
    total = ((RZ[0] + RZ[1]) + RZ[2]) + RZ[3]
    count = 1.0 / math.sqrt(TOK * 16)
    d_mean[...] = count * total[:, 0:HID]
    d_sigma[...] = count * a_noise[...] * total[:, HID : 2 * HID]
    d_factor[...] = (count * adapter_scale) * total[:, 2 * HID :]

    step_c(6)
    step_b(6)
    step_d(5)
    step_e(4)
    step_e(5)
    matmul(4, 2)
    step_d(6)
    finish(2)
    finish(3)
    step_e(6)
    matmul(6, 1)
    finish(4)
    finish(5)
    finish(6)

    landed(DW.at[pl.ds(0, 7)], send_dw)
    landed(OGP, send_og)
    landed(RSS, send_rs)
    landed(RVS.at[0], send_rv.at[0])
    for d in (1, 2, 3):
        landed(RVS.at[1], send_rv.at[d])
        landed(RY.at[y], send_ry.at[d - 1])
        landed(RZ.at[z], send_rz.at[d - 1])
    landed(RVS.at[2], send_rv.at[4])


def local(*args):
    vmem = pl.BlockSpec(memory_space=pltpu.VMEM)
    anywhere = pl.BlockSpec(memory_space=pl.ANY)
    dma = pltpu.SemaphoreType.DMA
    scratch = [
        pltpu.VMEM((8, HID, WID), BF16),
        pltpu.VMEM((2, TOK, HALF), BF16),
        pltpu.VMEM((2, TOK, HALF), BF16),
        pltpu.VMEM((2, TOK, HALF), BF16),
        pltpu.VMEM((TOK, WID), BF16),
        pltpu.VMEM((TOK, HID), BF16),
        pltpu.VMEM((TOK, HID), BF16),
        pltpu.VMEM((TOK, HID), jnp.int32),
        pltpu.VMEM((TOK, HID), BF16),
        pltpu.VMEM((TOK, HID), BF16),
        pltpu.VMEM((TOK, HID), F32),
        pltpu.VMEM((TOK, HID), F32),
        pltpu.VMEM((TOK, HID), F32),
        pltpu.VMEM((TOK, 2 * CH), F32),
        pltpu.VMEM((NCH, TOK, CH), BF16),
        pltpu.VMEM((NCH, TOK, CH), BF16),
        pltpu.VMEM((128, 4 * HALF), BF16),
        pltpu.VMEM((TOK, 128), BF16),
        pltpu.VMEM((128, HID), BF16),
        pltpu.VMEM((128, HID), BF16),
        pltpu.VMEM((8, TOK), F32),
        pltpu.VMEM((3, 8, TOK), F32),
        pltpu.VMEM((5, 8, TOK), F32),
        pltpu.VMEM((4, 8, RED), F32),
        pltpu.VMEM((4, 8, RED), F32),
        dma((9,)),
        dma(()),
        dma(()),
        dma(()),
        dma((5,)),
        dma((3,)),
        dma((3,)),
        dma((NCH,)),
        dma((2, NCH)),
        dma((2, NCH)),
        dma((2, 2, NCH)),
        dma((8, 2)),
        dma((NCH,)),
        dma((5,)),
        dma((3,)),
        dma((3,)),
    ]
    return pl.pallas_call(
        kernel,
        out_shape=(
            jax.ShapeDtypeStruct((TOK, HID), BF16),
            jax.ShapeDtypeStruct((TOK, HID), BF16),
            jax.ShapeDtypeStruct((8, HID), F32),
            jax.ShapeDtypeStruct((8, HID), F32),
            jax.ShapeDtypeStruct((8, WID), F32),
        ),
        in_specs=[anywhere] * 4 + [vmem] * 4 + [anywhere, vmem],
        out_specs=(vmem,) * 5,
        scratch_shapes=scratch,
        compiler_params=pltpu.CompilerParams(
            collective_id=0, has_side_effects=True, vmem_limit_bytes=58 * 2**20
        ),
        name="ffn_backward",
    )(*args)


def solution(mesh):
    placed = (
        P("fsdp", None),
        P("fsdp", "tp"),
        P("fsdp", "tp"),
        P("tp", "fsdp"),
        P(None, "tp"),
        P(None, "tp"),
        P(None, "tp"),
        P(),
        P("fsdp", "tp"),
        P("fsdp", None),
    )
    return jax.shard_map(
        local,
        mesh=mesh,
        in_specs=placed,
        out_specs=(P("fsdp", "tp"), P("fsdp", "tp"), P(None, "tp"), P(None, "tp"), P(None, "tp")),
        check_vma=False,
    )
```

time: 445 us -> 120 us (0.27); the launches traced: 439 us -> 119 us
  waiting for transfers between devices: 290 us -> 0 us
  Pallas kernels: 0 us -> 108 us
  blocking collectives: 90.5 us -> 0 us
  matrix products: 40.7 us -> 0 us
  between operations: 14.1 us -> 0.64 us
  local copies, waits for them, and re-layouts: 0.19 us -> 9.94 us
    all_gather x1 -> x0, waiting for transfers between devices: 152 us -> none  [local(): lax.all_gather(down_weight, 'fsdp', axis=1, tiled=True)]
    psum x1 -> x0, waiting for transfers between devices: 138 us -> none  [local(): lax.psum((mean_part, sigma_part, factor_part), 'fsdp')]
    pallas_call x0 -> x1, Pallas kernels: none -> 108 us  [local(): pl.pallas_call(kernel, out_shape=(jax.ShapeDtypeStruct((TOK, HID), BF16),...]
    psum x1 -> x0, blocking collectives: 90.5 us -> none  [local(): rank_values = lax.psum(rank_local, 'tp')]
    dot_general x9 -> x0, matrix products: 40.7 us -> none  [the longest x1 18.6 us: contract_last(): lax.dot_general(left_rows, right_rows, (((1,), (1,)), ((), ())), preferre...]
    unnamed x12 -> x6, local copies, waits for them, and re-layouts: 0.19 us -> 9.94 us
  transfers between devices with their start and end apart: 2 -> 0, of which waited for: 2 -> 0; matrix products, arithmetic and copies ran while one was open for 3% -> 0% of each run, Pallas kernels for 0% -> 0%
where the time goes in v1:
time: 120 us; the launch traced here: 119 us
  Pallas kernels  108 us (90%)
  local copies, waits for them, and re-layouts  9.94 us (8%)
    pallas_call x1, Pallas kernels, local(): pl.pallas_call(kernel, out_shape=(jax.ShapeDtypeStruct((TOK, HID), BF16),...  108 us
    unnamed x6, local copies, waits for them, and re-layouts  9.94 us

profile of v1, /device:TPU:64, one launch (start us, length us, event | category | flops | bytes accessed | tf_op | source)
XLA Modules:
  0.0 119.0 jit_solution(4039775100777162109)
XLA Ops:
  0.6 1.6 %copy.15.out_signs = s32[512,8]{1,0:T(8,128)} copy(s32[512,8]{0,1:T(8,128)} %param.19) | data formatting | bytes 32768 | tf_op args[9]
  2.2 108.5 %ffn_backward.1 = (bf16[512,896]{1,0:T(8,128)(2,1)}, bf16[512,896]{1,0:T(8,128)(2,1)}, f32[8,896]{1,0:T(8,128)}, f32[8,896]{1,0:T(8,128)}, f32[8,512]{1,0:T(8,128)}) custom-call(bf16[512,8192]{1,0:T(8,128)(2,1)} %og.1, bf16[512,896]{1,0:T(8,128)(2,1)} %gate.1, bf16[512,896]{1,0:T(8,128)(2,1)} %up.1, bf16[896,512]{1,0:T(8,128)(2,1)} %dw.1, f32[8,896]{1,0:T(8,128)} %a_mean.1, ...), custom_call_target="tpu_custom_call" | custom-call | tf_op jit(solution)/shard_map/ffn_backward/pallas_call | solution.py:480
  110.7 2.2 %copy.21 = bf16[512,896]{1,0:T(8,128)(2,1)} copy(bf16[512,896]{1,0:T(8,128)(2,1)} %get-tuple-element.10) | data formatting | bytes 1835008
  112.8 2.2 %copy.22 = bf16[512,896]{1,0:T(8,128)(2,1)} copy(bf16[512,896]{1,0:T(8,128)(2,1)} %get-tuple-element.11) | data formatting | bytes 1835008
  115.0 1.4 %copy.23 = f32[8,896]{1,0:T(8,128)} copy(f32[8,896]{1,0:T(8,128)} %get-tuple-element.12) | data formatting | bytes 57344
  116.4 1.4 %copy.24 = f32[8,896]{1,0:T(8,128)} copy(f32[8,896]{1,0:T(8,128)} %get-tuple-element.13) | data formatting | bytes 57344
  117.7 1.3 %copy.25 = f32[8,512]{1,0:T(8,128)} copy(f32[8,512]{1,0:T(8,128)} %get-tuple-element.14) | data formatting | bytes 32768

commit v2 on v1

--- a/solution.py
+++ b/solution.py
@@ -42,12 +42,12 @@
     gate,
     up,
     dw,
-    a_mean,
-    a_sigma,
-    a_noise,
-    factor,
+    a_mean_in,
+    a_sigma_in,
+    a_noise_in,
+    factor_in,
     in_signs,
-    out_signs,
+    out_signs_in,
     d_gate,
     d_up,
     d_mean,
@@ -73,12 +73,20 @@
     LT,
     R1,
     R2,
-    SO,
     RVS,
     RVR,
     RY,
     RZ,
+    a_mean,
+    a_sigma,
+    a_noise,
+    factor,
+    out_signs,
+    OM,
+    OS,
+    OF,
     local_sem,
+    out_sem,
     send_dw,
     send_og,
     send_rs,
@@ -130,15 +138,21 @@
         pltpu.make_async_copy(gate, G, local_sem.at[1]),
         pltpu.make_async_copy(up, U, local_sem.at[2]),
         pltpu.make_async_copy(in_signs, IS, local_sem.at[3]),
+        pltpu.make_async_copy(a_mean_in, a_mean, local_sem.at[4]),
+        pltpu.make_async_copy(a_sigma_in, a_sigma, local_sem.at[5]),
+        pltpu.make_async_copy(a_noise_in, a_noise, local_sem.at[6]),
+        pltpu.make_async_copy(out_signs_in, out_signs, local_sem.at[7]),
+        pltpu.make_async_copy(factor_in, factor, local_sem.at[8]),
     ]
+    early = len(local)
     for h in range(2):
         mine = pl.ds(pl.multiple_of((2 * h + par) * HALF, HALF), HALF)
         rest = pl.ds(pl.multiple_of((2 * h + 1 - par) * HALF, HALF), HALF)
-        local.append(pltpu.make_async_copy(og.at[:, mine], OGO.at[h], local_sem.at[4 + 2 * h]))
-        local.append(pltpu.make_async_copy(og.at[:, rest], OGX.at[h], local_sem.at[5 + 2 * h]))
+        local.append(pltpu.make_async_copy(og.at[:, mine], OGO.at[h], local_sem.at[9 + 2 * h]))
+        local.append(pltpu.make_async_copy(og.at[:, rest], OGX.at[h], local_sem.at[10 + 2 * h]))
     out_cols = pl.ds(pl.multiple_of(tj * WID, WID), WID)
-    local.append(pltpu.make_async_copy(og.at[:, out_cols], OGC, local_sem.at[8]))
-    for copy in local:
+    local.append(pltpu.make_async_copy(og.at[:, out_cols], OGC, local_sem.at[13]))
+    for copy in local[1:early]:
         copy.start()
 
     pl.semaphore_wait(barrier, len(partners))
@@ -188,11 +202,11 @@
         return DW.at[slot, pl.ds(k * CH + part * (CH // 2), CH // 2)]
 
     def step_z(k):
-        send(rows_of(own, k), rows_of(own, k), send_dw, rz.at[k], across)
+        send(dw.at[pl.ds(k * CH, CH)], rows_of(own, k), send_dw, rz.at[k], across)
 
     def step_a(k):
-        send(rows_of(own, k), rows_of(own, k), send_dw, ra.at[0, k], right)
-        send(rows_of(own, k), rows_of(own, k), send_dw, ra.at[1, k], left)
+        send(dw.at[pl.ds(k * CH, CH)], rows_of(own, k), send_dw, ra.at[0, k], right)
+        send(dw.at[pl.ds(k * CH, CH)], rows_of(own, k), send_dw, ra.at[1, k], left)
 
     def step_b(k):
         landed(rows_of(mirror, k), rz.at[k])
@@ -218,40 +232,54 @@
             for part in range(2):
                 landed(rows_of(h * 4 + ring(y, 2), k, part), rc.at[part, group, k])
 
-    def matmul(k, count):
-        rows = pl.ds(k * CH, count * CH)
-        cols = slice(k * CH, (k + count) * CH)
+    def part(src, acc, acc_cols, rows, low, high):
+        def body(m, carry):
+            py = ring(y, m + 3)
+            kcols = pl.ds(pl.multiple_of(py * WID, WID), WID)
+            acc[:, acc_cols] += nt(src[0, :, kcols], DW[py, rows, :]) + nt(src[1, :, kcols], DW[4 + py, rows, :])
+            return carry
+
+        lax.fori_loop(low // 2, high // 2, body, 0)
+
+    def to_pair(k, n):
+        RSS[k] = PACC[:, n * CH : (n + 1) * CH].astype(BF16)
+        send(RSS.at[k], RSR.at[k], send_rs, rr.at[k], pair)
+
+    def to_partner(k, count):
         wide = slice(0, count * CH)
         PACC[:, wide] = jnp.zeros((TOK, count * CH), F32)
-
-        def part(src, acc, acc_cols):
-            def body(s, carry):
-                kcols = pl.ds(pl.multiple_of(lax.rem(s, 4) * WID, WID), WID)
-                acc[:, acc_cols] += nt(src[lax.div(s, 4), :, kcols], DW[s, rows, :])
-                return carry
-
-            lax.fori_loop(0, 8, body, 0)
-
-        part(OGP, PACC, wide)
+        part(OGP, PACC, wide, pl.ds(k * CH, count * CH), 0, 8)
         for n in range(count):
-            RSS[k + n] = PACC[:, n * CH : (n + 1) * CH].astype(BF16)
-            send(RSS.at[k + n], RSR.at[k + n], send_rs, rr.at[k + n], pair)
-        part(OGO, OWN, cols)
+            to_pair(k + n, n)
+
+    def to_self(k, count):
+        part(OGO, OWN, slice(k * CH, (k + count) * CH), pl.ds(k * CH, count * CH), 0, 8)
+
+    out_copies = []
+
+    def put(src, dst):
+        copy = pltpu.make_async_copy(src, dst, out_sem.at[len(out_copies)])
+        copy.start()
+        out_copies.append(copy)
 
     def finish(k):
         cols = slice(k * CH, (k + 1) * CH)
         landed(RSR.at[k], rr.at[k])
         hidden_grad = OWN[:, cols] + RSR[k].astype(F32)
-        d_gate[:, cols] = (hidden_grad * CA[:, cols]).astype(BF16)
-        d_up[:, cols] = (hidden_grad * CB[:, cols]).astype(BF16)
+        G[:, cols] = (hidden_grad * CA[:, cols]).astype(BF16)
+        U[:, cols] = (hidden_grad * CB[:, cols]).astype(BF16)
+        put(G.at[:, pl.ds(k * CH, CH)], d_gate.at[:, pl.ds(k * CH, CH)])
+        put(U.at[:, pl.ds(k * CH, CH)], d_up.at[:, pl.ds(k * CH, CH)])
 
     step_p(0)
     step_p(1)
-    local[0].wait()
+    for k in range(NCH):
+        step_a(k)
     for k in range(NCH):
         step_z(k)
-        if k < 3:
-            step_a(k)
+    local[0].start()
+    for copy in local[early:]:
+        copy.start()
 
     for n in (1, 2, 3):
         local[n].wait()
@@ -270,34 +298,31 @@
 
     lax.fori_loop(0, NCH, pre, 0)
 
+    for n in range(4, early):
+        local[n].wait()
     spread = a_sigma[...] * a_noise[...]
     am = thirds(a_mean[...])
     sp = thirds(spread)
     gap = jnp.zeros((8, HID), F32)
     R1[...] = jnp.concatenate([am[0], am[1], am[2]] + [gap] * 13, axis=0).astype(BF16)
     R2[...] = jnp.concatenate([gap] * 4 + [sp[0], sp[1], sp[2]] + [gap] * 9, axis=0).astype(BF16)
-    eye = (
-        lax.broadcasted_iota(jnp.int32, (8, 8), 0) == lax.broadcasted_iota(jnp.int32, (8, 8), 1)
-    ).astype(F32)
-    SO[...] = nt(eye, out_signs[...].astype(F32))
+    sign_out = out_signs[...].astype(F32)
     both = (nt(H[...], R1[...]) + nt(HS[...], R2[...])).T
-    RVS[0] = (both[0:8] + both[8:16] + both[16:24]) + SO[...] * (
+    RVS[0] = (both[0:8] + both[8:16] + both[16:24]) + sign_out * (
         both[32:40] + both[40:48] + both[48:56]
     )
     send(RVS.at[0], RVR.at[0], send_rv.at[0], rv.at[0], sibling)
 
+    step_x(0)
     step_c(0)
-    step_a(3)
-    step_b(0)
-    step_x(0)
-
     sf = thirds(factor[...])
     SF[...] = jnp.concatenate(
         [sf[0], sf[1], sf[2]] + [jnp.zeros((8, 4 * HALF), F32)] * 13, axis=0
     ).astype(BF16)
+    for n in range(early, len(local)):
+        local[n].wait()
+    local[0].wait()
     LTF = None
-    for n in range(4, 9):
-        local[n].wait()
     for h in range(2):
         mine = pl.ds(pl.multiple_of((2 * h + par) * HALF, HALF), HALF)
         rest = pl.ds(pl.multiple_of((2 * h + 1 - par) * HALF, HALF), HALF)
@@ -305,16 +330,14 @@
         LTF = term if LTF is None else LTF + term
     turned = LTF.T
     rank_grad = adapter_scale * (turned[0:8] + turned[8:16] + turned[16:24])
-    signed = rank_grad * SO[...]
+    signed = rank_grad * sign_out
     rg = thirds(rank_grad)
     sg = thirds(signed)
 
+    step_x(1)
+    step_b(0)
     step_c(1)
-    step_a(4)
-    step_b(1)
-    step_d(0)
-    step_x(1)
-
+    step_c(2)
     landed(RVR.at[0], rv.at[0])
     RVS[1] = RVS[0] + RVR[0]
     for d in (1, 2, 3):
@@ -340,6 +363,7 @@
         [gap] * 8 + [sp[0], sp[1], sp[0], sp[1], sp[2], sp[0]] + [gap] * 2, axis=0
     ).astype(BF16)
 
+    step_b(1)
     def rank_terms(k, carry):
         cols = pl.ds(pl.multiple_of(k * CH, CH), CH)
         OWN[:, cols] = nn(LT[...], R1[:, cols]) + IS[:, cols].astype(F32) * nn(LT[...], R2[:, cols])
@@ -347,25 +371,14 @@
 
     lax.fori_loop(0, NCH, rank_terms, 0)
 
-    step_y(0)
-    step_c(2)
-    step_a(5)
-    step_b(2)
-    step_d(1)
-
     for d in (1, 2, 3):
         landed(RVR.at[d], rv.at[d])
     RVS[2] = RVS[1] + RVR[1] + RVR[2] + RVR[3]
     send(RVS.at[2], RVR.at[4], send_rv.at[4], rv.at[4], other_hi)
 
-    step_y(1)
-    step_w(0)
+    step_d(0)
     step_c(3)
-    step_a(6)
-    step_b(3)
-    step_d(2)
-    step_w(1)
-
+    step_b(2)
     landed(RVR.at[4], rv.at[4])
     ranks = thirds(RVS[2] + RVR[4])
     factor3 = nn(jnp.concatenate(list(ranks) + [blank], axis=0).astype(BF16), OGC[...])
@@ -373,50 +386,65 @@
     for d in (1, 2, 3):
         send(RY.at[y], RY.at[y], send_ry.at[d - 1], ry.at[d - 1], ys[d - 1])
 
+    step_y(0)
+    step_d(1)
+    step_c(4)
+    step_b(3)
+    step_d(2)
+    step_y(1)
     step_e(0)
     step_e(1)
-    matmul(0, 2)
-
-    step_c(4)
+    to_self(0, 2)
+    step_c(5)
     step_b(4)
     step_d(3)
-
+    step_w(0)
+    step_w(1)
+    to_partner(0, 2)
     for d in (1, 2, 3):
         landed(RY.at[ring(y, 4 - d)], ry.at[d - 1])
     RZ[z] = ((RY[0] + RY[1]) + RY[2]) + RY[3]
     for d in (1, 2, 3):
         send(RZ.at[z], RZ.at[z], send_rz.at[d - 1], rzz.at[d - 1], zs[d - 1])
 
+    step_c(6)
+    step_b(5)
+    step_d(4)
     step_e(2)
     step_e(3)
-    matmul(2, 2)
-    step_c(5)
-    step_b(5)
-    step_d(4)
-    finish(0)
-    finish(1)
-
+    to_partner(2, 2)
+    step_b(6)
+    step_d(5)
+    to_self(2, 2)
     for d in (1, 2, 3):
         landed(RZ.at[ring(z, 4 - d)], rzz.at[d - 1])
     total = ((RZ[0] + RZ[1]) + RZ[2]) + RZ[3]
     count = 1.0 / math.sqrt(TOK * 16)
-    d_mean[...] = count * total[:, 0:HID]
-    d_sigma[...] = count * a_noise[...] * total[:, HID : 2 * HID]
-    d_factor[...] = (count * adapter_scale) * total[:, 2 * HID :]
-
-    step_c(6)
-    step_b(6)
-    step_d(5)
+    OM[...] = count * total[:, 0:HID]
+    OS[...] = count * a_noise[...] * total[:, HID : 2 * HID]
+    OF[...] = (count * adapter_scale) * total[:, 2 * HID :]
+    put(OM, d_mean)
+    put(OS, d_sigma)
+    put(OF, d_factor)
+
+    step_d(6)
+    finish(0)
+    finish(1)
+    finish(2)
+    finish(3)
     step_e(4)
     step_e(5)
-    matmul(4, 2)
-    step_d(6)
-    finish(2)
-    finish(3)
+    to_partner(4, 2)
+    last = pl.ds(6 * CH, CH)
+    PACC[:, 0:CH] = jnp.zeros((TOK, CH), F32)
+    part(OGP, PACC, slice(0, CH), last, 0, 6)
     step_e(6)
-    matmul(6, 1)
+    part(OGP, PACC, slice(0, CH), last, 6, 8)
+    to_pair(6, 0)
+    to_self(4, 2)
     finish(4)
     finish(5)
+    to_self(6, 1)
     finish(6)
 
     landed(DW.at[pl.ds(0, 7)], send_dw)
@@ -428,10 +456,34 @@
         landed(RY.at[y], send_ry.at[d - 1])
         landed(RZ.at[z], send_rz.at[d - 1])
     landed(RVS.at[2], send_rv.at[4])
+    for copy in out_copies:
+        copy.wait()
+
+
+def hand_over(*refs):
+    sources, targets, held, sem = refs[:5], refs[5:10], refs[10:15], refs[15]
+    pieces = []
+    for n, parts in enumerate((4, 4, 1, 1, 1)):
+        step = sources[n].shape[0] // parts
+        for m in range(parts):
+            rows = pl.ds(m * step, step)
+            at = (sources[n].at[rows], held[n].at[rows], targets[n].at[rows])
+            pieces.append(
+                (
+                    pltpu.make_async_copy(at[0], at[1], sem.at[0, len(pieces)]),
+                    pltpu.make_async_copy(at[1], at[2], sem.at[1, len(pieces)]),
+                )
+            )
+    for inward, _ in pieces:
+        inward.start()
+    for inward, outward in pieces:
+        inward.wait()
+        outward.start()
+    for _, outward in pieces:
+        outward.wait()
 
 
 def local(*args):
-    vmem = pl.BlockSpec(memory_space=pltpu.VMEM)
     anywhere = pl.BlockSpec(memory_space=pl.ANY)
     dma = pltpu.SemaphoreType.DMA
     scratch = [
@@ -455,12 +507,20 @@
         pltpu.VMEM((TOK, 128), BF16),
         pltpu.VMEM((128, HID), BF16),
         pltpu.VMEM((128, HID), BF16),
-        pltpu.VMEM((8, TOK), F32),
         pltpu.VMEM((3, 8, TOK), F32),
         pltpu.VMEM((5, 8, TOK), F32),
         pltpu.VMEM((4, 8, RED), F32),
         pltpu.VMEM((4, 8, RED), F32),
-        dma((9,)),
+        pltpu.VMEM((8, HID), F32),
+        pltpu.VMEM((8, HID), F32),
+        pltpu.VMEM((8, HID), F32),
+        pltpu.VMEM((8, 4 * HALF), F32),
+        pltpu.VMEM((8, TOK), jnp.int32),
+        pltpu.VMEM((8, HID), F32),
+        pltpu.VMEM((8, HID), F32),
+        pltpu.VMEM((8, WID), F32),
+        dma((14,)),
+        dma((2 * NCH + 3,)),
         dma(()),
         dma(()),
         dma(()),
@@ -477,23 +537,32 @@
         dma((3,)),
         dma((3,)),
     ]
-    return pl.pallas_call(
+    shapes = (
+        jax.ShapeDtypeStruct((TOK, HID), BF16),
+        jax.ShapeDtypeStruct((TOK, HID), BF16),
+        jax.ShapeDtypeStruct((8, HID), F32),
+        jax.ShapeDtypeStruct((8, HID), F32),
+        jax.ShapeDtypeStruct((8, WID), F32),
+    )
+    results = pl.pallas_call(
         kernel,
-        out_shape=(
-            jax.ShapeDtypeStruct((TOK, HID), BF16),
-            jax.ShapeDtypeStruct((TOK, HID), BF16),
-            jax.ShapeDtypeStruct((8, HID), F32),
-            jax.ShapeDtypeStruct((8, HID), F32),
-            jax.ShapeDtypeStruct((8, WID), F32),
-        ),
-        in_specs=[anywhere] * 4 + [vmem] * 4 + [anywhere, vmem],
-        out_specs=(vmem,) * 5,
+        out_shape=shapes,
+        in_specs=[anywhere] * 10,
+        out_specs=(anywhere,) * 5,
         scratch_shapes=scratch,
         compiler_params=pltpu.CompilerParams(
             collective_id=0, has_side_effects=True, vmem_limit_bytes=58 * 2**20
         ),
         name="ffn_backward",
-    )(*args)
+    )(*args[:9], args[9].T)
+    return pl.pallas_call(
+        hand_over,
+        out_shape=shapes,
+        in_specs=[anywhere] * 5,
+        out_specs=(anywhere,) * 5,
+        scratch_shapes=[pltpu.VMEM(each.shape, each.dtype) for each in shapes] + [dma((2, 11))],
+        name="hand_over",
+    )(*results)
 
 
 def solution(mesh):

time: 120 us -> 101 us (0.84)
  local copies, waits for them, and re-layouts: 9.94 us -> 0 us
  Pallas kernels: 108 us -> 99.2 us
    unnamed x6 -> x0, local copies, waits for them, and re-layouts: 9.94 us -> none
    pallas_call x1 -> x2, Pallas kernels: 108 us -> 99.2 us  [the longest x1 96.7 us: local(): pl.pallas_call(kernel, out_shape=shapes, in_specs=[anywhere] * 10, out_sp...]
where the time goes in v2:
time: 101 us; the launch traced here: 99.9 us
  Pallas kernels  99.2 us (98%)
    pallas_call x1, Pallas kernels, local(): pl.pallas_call(kernel, out_shape=shapes, in_specs=[anywhere] * 10, out_sp...  96.7 us
    pallas_call x1, Pallas kernels, local(): pl.pallas_call(hand_over, out_shape=shapes, in_specs=[anywhere] * 5, out_...  2.47 us

profile of v2, /device:TPU:64, one launch (start us, length us, event | category | flops | bytes accessed | tf_op | source)
XLA Modules:
  0.0 99.9 jit_solution(11878486099023573876)
XLA Ops:
  0.6 96.7 %ffn_backward.1 = (bf16[512,896]{1,0:T(8,128)(2,1)}, bf16[512,896]{1,0:T(8,128)(2,1)}, f32[8,896]{1,0:T(8,128)}, f32[8,896]{1,0:T(8,128)}, f32[8,512]{1,0:T(8,128)}) custom-call(bf16[512,8192]{1,0:T(8,128)(2,1)} %og.1, bf16[512,896]{1,0:T(8,128)(2,1)} %gate.1, bf16[512,896]{1,0:T(8,128)(2,1)} %up.1, bf16[896,512]{1,0:T(8,128)(2,1)} %dw.1, ...), custom_call_target="tpu_custom_call" | custom-call | tf_op jit(solution)/shard_map/ffn_backward/pallas_call | solution.py:547
  97.4 2.5 %hand_over.1 = (bf16[512,896]{1,0:T(8,128)(2,1)}, bf16[512,896]{1,0:T(8,128)(2,1)}, f32[8,896]{1,0:T(8,128)}, f32[8,896]{1,0:T(8,128)}, f32[8,512]{1,0:T(8,128)}) custom-call(bf16[512,896]{1,0:T(8,128)(2,1)} %get-tuple-element.10.refs_0_, bf16[512,896]{1,0:T(8,128)(2,1)} %get-tuple-element.11.refs_1_, f32[8,896]{1,0:T(8,128)} %get-tuple-element.12.refs_2_, ...), custom_call_target="tpu_custom_call" | custom-call | tf_op jit(solution)/shard_map/hand_over/pallas_call | solution.py:558

commit v3 on v2

--- a/solution.py
+++ b/solution.py
@@ -98,6 +98,7 @@
     rb,
     rc,
     rp,
+    rh,
     rr,
     rv,
     ry,
@@ -182,14 +183,24 @@
 
     def step_x(h):
         landed(piece(q_own, h), rp.at[q_own, h])
-        for device in xs + [sibling]:
+        for device in (xs[0], xs[2], sibling):
             send(piece(q_own, h), piece(q_own, h), send_og, rp.at[q_own, h], device)
 
+    def half(q, h, side):
+        return OGP.at[h, pl.ds(pl.multiple_of(q * 64 + side * 32, 32), 32)]
+
     def step_y(h):
-        for d in (1, 3, 2):
+        for side, d in ((0, 3), (1, 1)):
             q = ring(x, d) * 2 + c
             landed(piece(q, h), rp.at[q, h])
+            send(half(q, h, side), half(q, h, side), send_og, rh.at[side, h], xs[(0, 2)[side]])
             send(piece(q, h), piece(q, h), send_og, rp.at[q, h], sibling)
+
+    def step_v(h):
+        q = ring(x, 2) * 2 + c
+        for side in range(2):
+            landed(half(q, h, side), rh.at[side, h])
+        send(piece(q, h), piece(q, h), send_og, rp.at[q, h], sibling)
 
     def step_w(h):
         for px in range(4):
@@ -254,6 +265,16 @@
 
     def to_self(k, count):
         part(OGO, OWN, slice(k * CH, (k + count) * CH), pl.ds(k * CH, count * CH), 0, 8)
+
+    def part_ry(slot, side):
+        return RY.at[slot, :, pl.ds(side * (RED // 2), RED // 2)]
+
+    def relay_ry():
+        for side, d in ((0, 3), (1, 1)):
+            slot = ring(y, d)
+            landed(RY.at[slot], ry.at[side])
+            onward = part_ry(slot, side)
+            send(onward, onward, send_ry.at[2 + side], ry.at[2 + side], (right, left)[side])
 
     out_copies = []
 
@@ -383,8 +404,8 @@
     ranks = thirds(RVS[2] + RVR[4])
     factor3 = nn(jnp.concatenate(list(ranks) + [blank], axis=0).astype(BF16), OGC[...])
     RY[y, :, 2 * HID :] = factor3[0:8] + factor3[8:16] + factor3[16:24]
-    for d in (1, 2, 3):
-        send(RY.at[y], RY.at[y], send_ry.at[d - 1], ry.at[d - 1], ys[d - 1])
+    send(RY.at[y], RY.at[y], send_ry.at[0], ry.at[0], right)
+    send(RY.at[y], RY.at[y], send_ry.at[1], ry.at[1], left)
 
     step_y(0)
     step_d(1)
@@ -398,24 +419,32 @@
     step_c(5)
     step_b(4)
     step_d(3)
+    relay_ry()
+    step_v(0)
+    step_c(6)
+    step_b(5)
+    step_v(1)
+    step_d(4)
     step_w(0)
     step_w(1)
     to_partner(0, 2)
-    for d in (1, 2, 3):
-        landed(RY.at[ring(y, 4 - d)], ry.at[d - 1])
+    step_e(2)
+    step_e(3)
+    to_partner(2, 2)
+    for side in range(2):
+        landed(part_ry(ring(y, 2), side), ry.at[2 + side])
     RZ[z] = ((RY[0] + RY[1]) + RY[2]) + RY[3]
     for d in (1, 2, 3):
         send(RZ.at[z], RZ.at[z], send_rz.at[d - 1], rzz.at[d - 1], zs[d - 1])
 
-    step_c(6)
-    step_b(5)
-    step_d(4)
-    step_e(2)
-    step_e(3)
-    to_partner(2, 2)
     step_b(6)
     step_d(5)
     to_self(2, 2)
+    step_d(6)
+    finish(0)
+    finish(1)
+    finish(2)
+    finish(3)
     for d in (1, 2, 3):
         landed(RZ.at[ring(z, 4 - d)], rzz.at[d - 1])
     total = ((RZ[0] + RZ[1]) + RZ[2]) + RZ[3]
@@ -427,11 +456,6 @@
     put(OS, d_sigma)
     put(OF, d_factor)
 
-    step_d(6)
-    finish(0)
-    finish(1)
-    finish(2)
-    finish(3)
     step_e(4)
     step_e(5)
     to_partner(4, 2)
@@ -453,9 +477,11 @@
     landed(RVS.at[0], send_rv.at[0])
     for d in (1, 2, 3):
         landed(RVS.at[1], send_rv.at[d])
-        landed(RY.at[y], send_ry.at[d - 1])
         landed(RZ.at[z], send_rz.at[d - 1])
     landed(RVS.at[2], send_rv.at[4])
+    for side in range(2):
+        landed(RY.at[y], send_ry.at[side])
+        landed(part_ry(y, side), send_ry.at[2 + side])
     for copy in out_copies:
         copy.wait()
 
@@ -525,16 +551,17 @@
         dma(()),
         dma(()),
         dma((5,)),
-        dma((3,)),
+        dma((4,)),
         dma((3,)),
         dma((NCH,)),
         dma((2, NCH)),
         dma((2, NCH)),
         dma((2, 2, NCH)),
         dma((8, 2)),
+        dma((2, 2)),
         dma((NCH,)),
         dma((5,)),
-        dma((3,)),
+        dma((4,)),
         dma((3,)),
     ]
     shapes = (

time: 101 us -> 96.9 us (0.959)
  Pallas kernels: 99.2 us -> 96.1 us
    pallas_call x1, Pallas kernels: 96.7 us -> 93.6 us  [local(): pl.pallas_call(kernel, out_shape=shapes, in_specs=[anywhere] * 10, out_sp...]
where the time goes in v3:
time: 96.9 us; the launch traced here: 96.7 us
  Pallas kernels  96.1 us (99%)
    pallas_call x1, Pallas kernels, local(): pl.pallas_call(kernel, out_shape=shapes, in_specs=[anywhere] * 10, out_sp...  93.6 us
    pallas_call x1, Pallas kernels, local(): pl.pallas_call(hand_over, out_shape=shapes, in_specs=[anywhere] * 5, out_...  2.47 us

profile of v3, /device:TPU:64, one launch (start us, length us, event | category | flops | bytes accessed | tf_op | source)
XLA Modules:
  0.0 96.7 jit_solution(17329052729714146677)
XLA Ops:
  0.6 93.6 %ffn_backward.1 = (bf16[512,896]{1,0:T(8,128)(2,1)}, bf16[512,896]{1,0:T(8,128)(2,1)}, f32[8,896]{1,0:T(8,128)}, f32[8,896]{1,0:T(8,128)}, f32[8,512]{1,0:T(8,128)}) custom-call(bf16[512,8192]{1,0:T(8,128)(2,1)} %og.1, bf16[512,896]{1,0:T(8,128)(2,1)} %gate.1, bf16[512,896]{1,0:T(8,128)(2,1)} %up.1, bf16[896,512]{1,0:T(8,128)(2,1)} %dw.1, ...), custom_call_target="tpu_custom_call" | custom-call | tf_op jit(solution)/shard_map/ffn_backward/pallas_call | solution.py:574
  94.3 2.5 %hand_over.1 = (bf16[512,896]{1,0:T(8,128)(2,1)}, bf16[512,896]{1,0:T(8,128)(2,1)}, f32[8,896]{1,0:T(8,128)}, f32[8,896]{1,0:T(8,128)}, f32[8,512]{1,0:T(8,128)}) custom-call(bf16[512,896]{1,0:T(8,128)(2,1)} %get-tuple-element.10.refs_0_, bf16[512,896]{1,0:T(8,128)(2,1)} %get-tuple-element.11.refs_1_, f32[8,896]{1,0:T(8,128)} %get-tuple-element.12.refs_2_, ...), custom_call_target="tpu_custom_call" | custom-call | tf_op jit(solution)/shard_map/hand_over/pallas_call | solution.py:585

commit v4 on v3

--- a/solution.py
+++ b/solution.py
@@ -443,8 +443,6 @@
     step_d(6)
     finish(0)
     finish(1)
-    finish(2)
-    finish(3)
     for d in (1, 2, 3):
         landed(RZ.at[ring(z, 4 - d)], rzz.at[d - 1])
     total = ((RZ[0] + RZ[1]) + RZ[2]) + RZ[3]
@@ -459,6 +457,8 @@
     step_e(4)
     step_e(5)
     to_partner(4, 2)
+    finish(2)
+    finish(3)
     last = pl.ds(6 * CH, CH)
     PACC[:, 0:CH] = jnp.zeros((TOK, CH), F32)
     part(OGP, PACC, slice(0, CH), last, 0, 6)

time: 96.9 us -> 96.9 us (level)
  no operation moved by 1% of the time
where the time goes in v4:
time: 96.9 us; the launch traced here: 96.7 us
  Pallas kernels  96.1 us (99%)
    pallas_call x1, Pallas kernels, local(): pl.pallas_call(kernel, out_shape=shapes, in_specs=[anywhere] * 10, out_sp...  93.6 us
    pallas_call x1, Pallas kernels, local(): pl.pallas_call(hand_over, out_shape=shapes, in_specs=[anywhere] * 5, out_...  2.47 us

profile of v4, /device:TPU:64, one launch (start us, length us, event | category | flops | bytes accessed | tf_op | source)
XLA Modules:
  0.0 96.7 jit_solution(2962735489500314002)
XLA Ops:
  0.6 93.6 %ffn_backward.1 = (bf16[512,896]{1,0:T(8,128)(2,1)}, bf16[512,896]{1,0:T(8,128)(2,1)}, f32[8,896]{1,0:T(8,128)}, f32[8,896]{1,0:T(8,128)}, f32[8,512]{1,0:T(8,128)}) custom-call(bf16[512,8192]{1,0:T(8,128)(2,1)} %og.1, bf16[512,896]{1,0:T(8,128)(2,1)} %gate.1, bf16[512,896]{1,0:T(8,128)(2,1)} %up.1, bf16[896,512]{1,0:T(8,128)(2,1)} %dw.1, ...), custom_call_target="tpu_custom_call" | custom-call | tf_op jit(solution)/shard_map/ffn_backward/pallas_call | solution.py:574
  94.3 2.5 %hand_over.1 = (bf16[512,896]{1,0:T(8,128)(2,1)}, bf16[512,896]{1,0:T(8,128)(2,1)}, f32[8,896]{1,0:T(8,128)}, f32[8,896]{1,0:T(8,128)}, f32[8,512]{1,0:T(8,128)}) custom-call(bf16[512,896]{1,0:T(8,128)(2,1)} %get-tuple-element.10.refs_0_, bf16[512,896]{1,0:T(8,128)(2,1)} %get-tuple-element.11.refs_1_, f32[8,896]{1,0:T(8,128)} %get-tuple-element.12.refs_2_, ...), custom_call_target="tpu_custom_call" | custom-call | tf_op jit(solution)/shard_map/hand_over/pallas_call | solution.py:585
